TPU v7x, 512 devices: a whole 4x4x16 slice. The times are simulated.
512 devices in a mesh: gx: 32 (over z, core), gy: 16 (over y, x).
Axes of the slice: x: 4, y: 4, z: 16, core: 2. Of those that a mesh axis runs over, the one named last changes fastest.
Arguments:
- solution: float32 [512, 65536], P(None, ('gx', 'gy')), may hold values from -6 to 6
- residual: float32 [512, 65536], P(None, ('gx', 'gy')), may hold values from -60 to 60
- metric_diag: bfloat16 [3, 512, 65536], P(None, None, ('gx', 'gy')), may hold values from 0.039794922 to 0.3984375
- metric_cross: bfloat16 [3, 512, 65536], P(None, None, ('gx', 'gy')), may hold values from -0.017944336 to 0.017944336
- fdm_vectors: float32 [3, 8, 8, 65536], P(None, None, None, ('gx', 'gy')), may hold values from -5 to 5
- fdm_values: float32 [3, 8, 65536], P(None, None, ('gx', 'gy')), may hold values from 0.05 to 20
- vertex_ids: int32 [8, 65536], P(None, ('gx', 'gy')), may hold values from 0 to 8191
- coarse_inverse: float32 [8192, 8192], P(('gx', 'gy')), may hold values from -0.2 to 0.2, as said below
- elem_live: int32 [512], P(('gx', 'gy')), may hold values from 80 to 128, as said below
- section_face: int32 [512, 16, 20], P(('gx', 'gy')), may hold values from -1 to 767, as said below
- section_code: int32 [512, 16, 20], P(('gx', 'gy')), may hold values from 0 to 7, as said below
- pipe_face: int32 [512, 2, 64], P(('gx', 'gy')), may hold values from 0 to 767, as said below
- pipe_code: int32 [512, 2, 64], P(('gx', 'gy')), may hold values from 0 to 7, as said below
Outputs:
- solution_out: float32 [512, 65536], P(None, ('gx', 'gy'))
- residual_out: float32 [512, 65536], P(None, ('gx', 'gy'))
- norm_ratio: float32 [1], replicated
Inputs may be any that keep to these rules, and one draw needn't show every extreme that they name: `elem_live`: one device holds all 128 slots in every draw. A face id 6 e + f names face f of slot e of the device, with e below the device's elem_live; no id appears twice on a device over section_face and pipe_face; -1 marks an empty slot, and in each peer's row the slots holding faces come first. Slot (q, c) of device (x, y) holds a face exactly when slot (y, c) of device (x, q) does; in the row q = y they come in pairs (c, c xor 1). Each device's rows for peers y - 1, y + 1 and y + 16 / 2 (mod 16) are full; rows for other peers more than two places away (mod 16) are empty. `section_code`: with inv(o) = o for o < 4 and 4 + 2 (o mod 2) + floor((o mod 4) / 2) for o >= 4, the codes of two paired slots are inv of each other; empty slots hold 0. `pipe_face`: every slot holds a face, as for section_face. `pipe_code`: the codes of two paired slots are inv of each other, as for section_code. `coarse_inverse`: Symmetric.
All inputs are finite; a program needn't handle non-finite values.
Results may differ from a plain program's by a relative error of at most 0.0003.
Values sent between devices are 32-bit elements; how exact they have to be, the bound alone decides.
A program may use at most 64 MiB of HBM per device.

v0:
```python
import jax
import jax.numpy as jnp
from jax import lax
from jax.sharding import PartitionSpec as P

EDGE = 8
top_precision = lax.Precision.HIGHEST


def padded(block, sides, width):
    for axis, dim in sides:
        count = lax.axis_size(axis)
        forward = [(i, i + 1) for i in range(count - 1)]
        forward.append((count - 1, 0))
        backward = [(target, source) for source, target in forward]
        low = lax.ppermute(
            lax.slice_in_dim(block, block.shape[dim] - width, None, axis=dim), axis, forward
        )
        high = lax.ppermute(lax.slice_in_dim(block, 0, width, axis=dim), axis, backward)
        block = jnp.concatenate([low, block, high], axis=dim)
    return block


def node_points():
    node_index = jnp.arange(EDGE).astype(jnp.float32)
    return -jnp.cos(jnp.pi * node_index / (EDGE - 1))


def derivative_matrix():
    points = node_points()
    node_index = jnp.arange(EDGE)
    weights = jnp.where((node_index == 0) | (node_index == EDGE - 1), 2.0, 1.0).astype(jnp.float32)
    parity = jnp.where((node_index[:, None] + node_index[None, :]) % 2 == 0, 1.0, -1.0).astype(
        jnp.float32
    )
    identity = jnp.eye(EDGE, dtype=jnp.float32)
    spacing = points[:, None] - points[None, :] + identity
    offdiag = weights[:, None] / weights[None, :] * parity / spacing * (1.0 - identity)
    return offdiag - jnp.diag(jnp.sum(offdiag, axis=1))


def corner_table():
    points = node_points()
    hat_values = jnp.stack([(1.0 - points) * 0.5, (1.0 + points) * 0.5])
    corner_weights = (
        hat_values[:, None, None, :, None, None]
        * hat_values[None, :, None, None, :, None]
        * hat_values[None, None, :, None, None, :]
    )
    return corner_weights.reshape(8, EDGE**3)


def contract(matrices, element_cube, axis):
    moved = jnp.moveaxis(element_cube, axis, 0)
    total = matrices[0][:, None, None, :] * moved[0][None]
    for index in range(1, EDGE):
        total = total + matrices[index][:, None, None, :] * moved[index][None]
    return jnp.moveaxis(total, 0, axis)


def orient_columns(face_cols, orient_codes):
    face_grid = face_cols.reshape(EDGE, EDGE, -1)
    face_grid = jnp.where((orient_codes % 2 == 1)[None, None, :], face_grid[::-1, :, :], face_grid)
    face_grid = jnp.where(
        (orient_codes // 2 % 2 == 1)[None, None, :], face_grid[:, ::-1, :], face_grid
    )
    face_grid = jnp.where(
        (orient_codes >= 4)[None, None, :], jnp.swapaxes(face_grid, 0, 1), face_grid
    )
    return face_grid.reshape(EDGE * EDGE, -1)


def fdm_solve(element_cube, vectors, values):
    spectral = contract(vectors[0], element_cube, 0)
    spectral = contract(vectors[1], spectral, 1)
    spectral = contract(vectors[2], spectral, 2)
    eigen_sums = (
        values[0][:, None, None, :] + values[1][None, :, None, :] + values[2][None, None, :, :]
    )
    spectral = spectral / eigen_sums
    restored = contract(jnp.swapaxes(vectors[0], 0, 1), spectral, 0)
    restored = contract(jnp.swapaxes(vectors[1], 0, 1), restored, 1)
    return contract(jnp.swapaxes(vectors[2], 0, 1), restored, 2)


def local_operator(field, diag_part, cross_part, derivative):
    element_cube = field.reshape(EDGE, EDGE, EDGE, -1)
    diagonal = diag_part.astype(jnp.float32).reshape(3, EDGE, EDGE, EDGE, -1)
    cross_terms = cross_part.astype(jnp.float32).reshape(3, EDGE, EDGE, EDGE, -1)
    forward = jnp.transpose(derivative)[:, :, None]
    backward = derivative[:, :, None]
    grad_first = contract(forward, element_cube, 0)
    grad_second = contract(forward, element_cube, 1)
    grad_third = contract(forward, element_cube, 2)
    flux_first = (
        diagonal[0] * grad_first + cross_terms[0] * grad_second + cross_terms[1] * grad_third
    )
    flux_second = (
        cross_terms[0] * grad_first + diagonal[1] * grad_second + cross_terms[2] * grad_third
    )
    flux_third = (
        cross_terms[1] * grad_first + cross_terms[2] * grad_second + diagonal[2] * grad_third
    )
    curvature = jnp.sum(
        grad_first * flux_first + grad_second * flux_second + grad_third * flux_third
    ) + jnp.sum(element_cube * element_cube)
    applied = contract(backward, flux_first, 0)
    applied = applied + contract(backward, flux_second, 1)
    applied = applied + contract(backward, flux_third, 2)
    return ((applied + element_cube).reshape(EDGE**3, -1), curvature)


def face_sum(field, section_face, section_code, pipe_face, pipe_code):
    element_cube = field.reshape(EDGE, EDGE, EDGE, -1)
    slot_count = element_cube.shape[3]
    stacked = jnp.stack(
        [
            element_cube[0],
            element_cube[EDGE - 1],
            element_cube[:, 0],
            element_cube[:, EDGE - 1],
            element_cube[:, :, 0],
            element_cube[:, :, EDGE - 1],
        ],
        axis=-1,
    )
    face_values = stacked.reshape(EDGE * EDGE, slot_count * 6)
    face_count = face_values.shape[1]
    peer_count = section_face.shape[1]
    capacity = section_face.shape[2]
    wanted = section_face[0].reshape(-1)
    picked = jnp.take(face_values, jnp.maximum(wanted, 0), axis=1)
    outgoing = jnp.where((wanted >= 0)[None, :], picked, 0.0).reshape(
        EDGE * EDGE, peer_count, capacity
    )
    own_index = lax.axis_index("gy")
    arrived = lax.all_to_all(outgoing, "gy", split_axis=1, concat_axis=1, tiled=True)
    swapped = arrived.reshape(EDGE * EDGE, peer_count, capacity // 2, 2)[..., ::-1].reshape(
        EDGE * EDGE, peer_count, capacity
    )
    arrived = jnp.where((jnp.arange(peer_count) == own_index)[None, :, None], swapped, arrived)
    incoming = orient_columns(
        arrived.reshape(EDGE * EDGE, peer_count * capacity), section_code[0].reshape(-1)
    )
    pipe_ids = pipe_face[0]
    pipe_width = pipe_ids.shape[1]
    boundary = jnp.take(face_values, pipe_ids.reshape(-1), axis=1).reshape(
        EDGE * EDGE, 2, pipe_width
    )
    extended = padded(boundary, (("gx", 1),), 1)
    beside = jnp.concatenate([extended[:, 0], extended[:, 3]], axis=1)
    beside = orient_columns(beside, pipe_code[0].reshape(-1))
    targets = jnp.concatenate([wanted, pipe_ids.reshape(-1)])
    placed = jnp.where(targets < 0, face_count, targets)
    face_extra = (
        jnp.zeros((EDGE * EDGE, face_count), jnp.float32)
        .at[:, placed]
        .add(jnp.concatenate([incoming, beside], axis=1), mode="drop")
    )
    face_parts = face_extra.reshape(EDGE, EDGE, slot_count, 6)
    element_cube = element_cube.at[0].add(face_parts[..., 0])
    element_cube = element_cube.at[EDGE - 1].add(face_parts[..., 1])
    element_cube = element_cube.at[:, 0].add(face_parts[..., 2])
    element_cube = element_cube.at[:, EDGE - 1].add(face_parts[..., 3])
    element_cube = element_cube.at[:, :, 0].add(face_parts[..., 4])
    element_cube = element_cube.at[:, :, EDGE - 1].add(face_parts[..., 5])
    return element_cube.reshape(EDGE**3, -1)


def on_device(
    solution,
    residual,
    metric_diag,
    metric_cross,
    fdm_vectors,
    fdm_values,
    vertex_ids,
    coarse_inverse,
    elem_live,
    section_face,
    section_code,
    pipe_face,
    pipe_code,
):
    slot_count = residual.shape[1]
    alive_mask = (jnp.arange(slot_count) < elem_live[0]).astype(jnp.float32)
    rmask = residual * alive_mask[None, :]
    corner_weights = corner_table()
    derivative = derivative_matrix()
    corners = jnp.dot(corner_weights, rmask, precision=top_precision)
    coarse_partial = jax.ops.segment_sum(
        corners.reshape(-1), vertex_ids.reshape(-1), num_segments=coarse_inverse.shape[1]
    )
    coarse_rhs = lax.psum(coarse_partial, ("gx", "gy"))
    own_values = jnp.dot(coarse_inverse, coarse_rhs, precision=top_precision)
    coarse_sol = lax.all_gather(own_values, ("gx", "gy"), axis=0, tiled=True)
    smooth = fdm_solve(rmask.reshape(EDGE, EDGE, EDGE, -1), fdm_vectors, fdm_values).reshape(
        EDGE**3, -1
    )
    summed = face_sum(smooth, section_face, section_code, pipe_face, pipe_code)
    lifted = jnp.dot(corner_weights.T, coarse_sol[vertex_ids], precision=top_precision)
    direction = alive_mask[None, :] * (summed + lifted)
    applied, curvature_local = local_operator(direction, metric_diag, metric_cross, derivative)
    image = face_sum(applied, section_face, section_code, pipe_face, pipe_code)
    precond_local = jnp.sum(rmask * direction)
    norm_local = jnp.sum(rmask * rmask)
    precond_dot, curvature, old_norm = lax.psum(
        (precond_local, curvature_local, norm_local), ("gx", "gy")
    )
    step_length = precond_dot / curvature
    residual_out = rmask - step_length * image
    fresh_norm = lax.psum(jnp.sum(residual_out * residual_out), ("gx", "gy"))
    solution_out = alive_mask[None, :] * (solution + step_length * direction)
    norm_ratio = (fresh_norm / old_norm).reshape(1)
    return (solution_out, residual_out, norm_ratio)


def solution(mesh):
    placed = (
        P(None, ("gx", "gy")),
        P(None, ("gx", "gy")),
        P(None, None, ("gx", "gy")),
        P(None, None, ("gx", "gy")),
        P(None, None, None, ("gx", "gy")),
        P(None, None, ("gx", "gy")),
        P(None, ("gx", "gy")),
        P(("gx", "gy"), None),
        P(("gx", "gy")),
        P(("gx", "gy"), None, None),
        P(("gx", "gy"), None, None),
        P(("gx", "gy"), None, None),
        P(("gx", "gy"), None, None),
    )
    return jax.shard_map(
        on_device,
        mesh=mesh,
        in_specs=placed,
        out_specs=(P(None, ("gx", "gy")), P(None, ("gx", "gy")), P()),
        check_vma=False,
    )
```

profile of v0, /device:TPU:1, one launch (start us, length us, event | category | flops | bytes accessed | tf_op | source)
XLA Modules:
  0.0 567.3 jit_solution(12377010773833954774)
XLA Ops:
  0.7 0.9 slice_bitcast_fusion.120
  2.3 0.8 slice_bitcast_fusion.92
  3.8 1.0 broadcast_multiply_fusion.3
  6.8 2.3 copy.389
  9.0 2.5 reshape.1869
  12.5 1.1 gather_fusion.1
  14.6 7.6 %all-to-all-start = ((f32[16,1,1280]{2,1,0:T(1,128)}), f32[16,1,1280]{2,1,0:T(1,128)}, u32[]{:S(2)}, u32[]{:S(2)}) async-start(f32[16,1,1280]{2,1,0:T(1,128)} %reshape.1990), calls=%async_computation | async-start | bytes 163840 | tf_op jit(solution)/shard_map/all_to_all | solution.py:137
  23.7 2.5 collective-permute-start
  26.8 0.9 collective-permute-start.1
  30.1 5.9 %scatter_custom_fusion.1 = f32[8192]{0:T(1024)S(1)} fusion(s32[1024]{0:T(1024)S(1)} %bitcast.649, f32[1024]{0:T(1024)S(1)} %convolution_bitcast_fusion, f32[]{:T(128)} %constant.402.clone.1), kind=kCustom, calls=%fused_computation.199 | custom fusion | flops 1024 | bytes 32772 | tf_op jit(solution)/shard_map/scatter-add | solution.py:191
  36.1 108.5 %psum.35 = f32[8192]{0:T(1024)S(1)} all-reduce(f32[8192]{0:T(1024)S(1)} %scatter_custom_fusion.1), channel_id=1, replica_groups=mesh['gx'=32,'gy'=16] {'gx','gy'}, use_global_device_ids=true, to_apply=%region_2.5 | all-reduce | flops 8192 | bytes 65536 | tf_op jit(solution)/shard_map/psum | solution.py:194
  145.0 1.0 fusion.56
  145.9 1.0 fusion.55
  169.9 99.5 %all-reduce = f32[8192]{0:T(1024)S(1)} all-reduce(f32[8192]{0:T(1024)S(1)} %dynamic-update-slice.36), channel_id=1, replica_groups=mesh['gx'=32,'gy'=16] {'gx','gy'}, use_global_device_ids=true, to_apply=%add | all-reduce | flops 8192 | bytes 65536
  269.4 10.5 %gather_fusion = f32[1024]{0:T(1024)} fusion(f32[8192]{0:T(1024)S(1)} %all-reduce, s32[1024]{0:T(1024)S(1)} %fusion.40), kind=kCustom, calls=%fused_computation.4 | custom fusion | bytes 12288 | tf_op jit(solution)/shard_map/gather | solution.py:201
  280.6 1.6 reduce.26
  283.5 2.3 scatter_custom_fusion
  285.7 2.6 reshape.1876
  288.4 3.4 fusion.54
  291.8 1.9 copy.456
  293.6 0.8 copy.457
  294.4 1.3 copy.401
  295.7 1.2 copy.403
  296.9 1.2 copy.458
  298.1 1.2 copy.459
  299.4 0.9 fusion.25
  301.8 2.0 multiply_reduce_fusion
  304.4 1.5 multiply_add_fusion
  306.1 1.5 add_bitcast_fusion.1
  309.7 2.3 copy.428
  312.0 2.4 reshape.1886
  314.4 1.1 gather_fusion.3
  317.3 4.2 all-to-all-start.1
  322.3 1.8 collective-permute-start.2
  324.9 0.8 mul.2645
  325.9 0.8 mul.2653
  326.7 0.8 mul.2661
  339.6 2.9 add_reduce_fusion
  343.7 102.5 %all-reduce.2 = (f32[]{:T(128)}, f32[]{:T(128)}) all-reduce(f32[]{:T(128)} %get-tuple-element.150, f32[]{:T(128)S(6)} %add.970), channel_id=1, replica_groups=mesh['gx'=32,'gy'=16] {'gx','gy'}, use_global_device_ids=true, to_apply=%region_4.7 | all-reduce | flops 2 | bytes 16 | tf_op jit(solution)/shard_map/psum | solution.py:207
  447.6 1.7 add_multiply_fusion
  449.3 0.9 pad_maximum_fusion.1
  450.2 1.6 reduce.27
  453.1 2.5 scatter_custom_fusion.2
  455.7 2.6 reshape.1893
  458.3 2.9 fusion.53
  461.2 1.2 copy.462
  464.1 1.3 multiply_reduce_fusion.1
  465.4 99.4 %all-reduce.1 = (f32[]{:T(128)}, f32[]{:T(128)}) all-reduce(f32[]{:T(128)} %get-tuple-element.156, f32[]{:T(128)} %get-tuple-element.149), channel_id=1, replica_groups=mesh['gx'=32,'gy'=16] {'gx','gy'}, use_global_device_ids=true, to_apply=%region_11.14 | all-reduce | flops 2 | bytes 16 | tf_op jit(solution)/shard_map/psum | solution.py:212
  (499 shorter events, 55.4 us)
Async XLA Ops:
  0.6 147.6 %copy-start = (f32[16,8192]{1,0:T(8,128)S(1)}, f32[16,8192]{1,0:T(8,128)}, u32[]{:S(2)}) copy-start(f32[16,8192]{1,0:T(8,128)} %param.48) | copy-start | bytes 1572868
  9.0 13.9 %copy-start.124 = (s32[1,2,64]{2,1,0:T(2,128)S(1)}, s32[1,2,64]{2,1,0:T(2,128)}, u32[]{:S(2)}) copy-start(s32[1,2,64]{2,1,0:T(2,128)} %param.53) | copy-start | bytes 1540
  9.0 21.1 %copy-start.121 = (s32[8,128]{1,0:T(8,128)S(1)}, s32[8,128]{1,0:T(8,128)}, u32[]{:S(2)}) copy-start(s32[8,128]{1,0:T(8,128)} %param.47) | copy-start | bytes 12292
  9.0 135.9 %copy-start.2 = (bf16[3,512,128]{2,1,0:T(8,128)(2,1)S(1)}, bf16[3,512,128]{2,1,0:T(8,128)(2,1)}, u32[]{:S(2)}) copy-start(bf16[3,512,128]{2,1,0:T(8,128)(2,1)} %param.44) | copy-start | bytes 1179652
  11.5 134.5 %copy-start.1 = (bf16[3,512,128]{2,1,0:T(8,128)(2,1)S(1)}, bf16[3,512,128]{2,1,0:T(8,128)(2,1)}, u32[]{:S(2)}) copy-start(bf16[3,512,128]{2,1,0:T(8,128)(2,1)} %param.43) | copy-start | bytes 1179652
  12.5 134.4 %copy-start.110 = (s32[1024]{0:T(1024)}, s32[1024]{0:T(1024)S(1)}, u32[]{:S(2)}) copy-start(s32[1024]{0:T(1024)S(1)} %get-tuple-element.373) | copy-start | bytes 12292
  14.6 265.5 %all-to-all-start = ((f32[16,1,1280]{2,1,0:T(1,128)}), f32[16,1,1280]{2,1,0:T(1,128)}, u32[]{:S(2)}, u32[]{:S(2)}) async-start(f32[16,1,1280]{2,1,0:T(1,128)} %reshape.1990), calls=%async_computation | async-start | bytes 163840 | tf_op jit(solution)/shard_map/all_to_all | solution.py:137
  23.5 256.5 %copy-start.66 = (pred[128]{0:T(512)(128)(4,1)}, pred[128]{0:T(512)(128)(4,1)S(1)}, u32[]{:S(2)}) copy-start(pred[128]{0:T(512)(128)(4,1)S(1)} %get-tuple-element.360) | copy-start | bytes 388
  23.7 256.2 %collective-permute-start = (f32[64,1,64]{2,0,1:T(8,128)S(1)}, f32[64,1,64]{2,0,1:T(8,128)S(1)}, u32[]{:S(2)}, u32[]{:S(2)}) collective-permute-start(f32[64,1,64]{2,0,1:T(8,128)S(1)} %copy.454), channel_id=1, source_target_pairs={{0,16},{16,32},{32,48},{48,64},{64,80},{80,96},{96,112},{112,128},... | collective-permute-start | bytes 49160 | tf_op jit(solution)/shard_map/ppermute | solution.py:16
  26.8 253.1 %collective-permute-start.1 = (f32[64,1,64]{2,0,1:T(8,128)}, f32[64,1,64]{2,0,1:T(8,128)S(1)}, u32[]{:S(2)}, u32[]{:S(2)}) collective-permute-start(f32[64,1,64]{2,0,1:T(8,128)} %copy.455), channel_id=1, source_target_pairs={{16,0},{32,16},{48,32},{64,48},{80,64},{96,80},{112,96},{128,112},... | collective-permute-start | bytes 49160 | tf_op jit(solution)/shard_map/ppermute | solution.py:19
  144.9 19.5 %copy-start.42 = (f32[8]{0:T(128)}, f32[8]{0:T(128)S(1)}, u32[]{:S(2)}) copy-start(f32[8]{0:T(128)S(1)} %get-tuple-element.346) | copy-start | bytes 100
  144.9 20.1 %copy-start.56 = (f32[8]{0:T(128)}, f32[8]{0:T(128)S(1)}, u32[]{:S(2)}) copy-start(f32[8]{0:T(128)S(1)} %get-tuple-element.353) | copy-start | bytes 100
  144.9 20.8 %copy-start.54 = (f32[8]{0:T(128)}, f32[8]{0:T(128)S(1)}, u32[]{:S(2)}) copy-start(f32[8]{0:T(128)S(1)} %get-tuple-element.352) | copy-start | bytes 100
  144.9 21.4 %copy-start.52 = (f32[8]{0:T(128)}, f32[8]{0:T(128)S(1)}, u32[]{:S(2)}) copy-start(f32[8]{0:T(128)S(1)} %get-tuple-element.351) | copy-start | bytes 100
  144.9 22.1 %copy-start.50 = (f32[8]{0:T(128)}, f32[8]{0:T(128)S(1)}, u32[]{:S(2)}) copy-start(f32[8]{0:T(128)S(1)} %get-tuple-element.350) | copy-start | bytes 100
  144.9 22.8 %copy-start.48 = (f32[8]{0:T(128)}, f32[8]{0:T(128)S(1)}, u32[]{:S(2)}) copy-start(f32[8]{0:T(128)S(1)} %get-tuple-element.349) | copy-start | bytes 100
  144.9 23.5 %copy-start.46 = (f32[8]{0:T(128)}, f32[8]{0:T(128)S(1)}, u32[]{:S(2)}) copy-start(f32[8]{0:T(128)S(1)} %get-tuple-element.348) | copy-start | bytes 100
  145.0 24.1 %copy-start.44 = (f32[8]{0:T(128)}, f32[8]{0:T(128)S(1)}, u32[]{:S(2)}) copy-start(f32[8]{0:T(128)S(1)} %get-tuple-element.347) | copy-start | bytes 100
  152.5 127.5 %copy-start.83 = (pred[128]{0:T(512)(128)(4,1)S(1)}, pred[128]{0:T(512)(128)(4,1)}, u32[]{:S(2)}) copy-start(pred[128]{0:T(512)(128)(4,1)} %get-tuple-element.361) | copy-start | bytes 388
  152.6 127.5 %copy-start.117 = (pred[128]{0:T(512)(128)(4,1)S(1)}, pred[128]{0:T(512)(128)(4,1)}, u32[]{:S(2)}) copy-start(pred[128]{0:T(512)(128)(4,1)} %get-tuple-element.359) | copy-start | bytes 388
  165.0 117.4 %copy-start.122 = (pred[16]{0:T(512)(128)(4,1)S(1)}, pred[16]{0:T(512)(128)(4,1)}, u32[]{:S(2)}) copy-start(pred[16]{0:T(512)(128)(4,1)} %iota_compare_fusion.2) | copy-start | bytes 52
  269.4 13.6 %copy-start.64 = (pred[320]{0:T(512)(128)(4,1)S(1)}, pred[320]{0:T(512)(128)(4,1)}, u32[]{:S(2)}) copy-start(pred[320]{0:T(512)(128)(4,1)} %get-tuple-element.355) | copy-start | bytes 964
  269.4 13.8 %copy-start.73 = (pred[320]{0:T(512)(128)(4,1)S(1)}, pred[320]{0:T(512)(128)(4,1)}, u32[]{:S(2)}) copy-start(pred[320]{0:T(512)(128)(4,1)} %get-tuple-element.356) | copy-start | bytes 964
  269.4 13.8 %copy-start.111 = (pred[320]{0:T(512)(128)(4,1)S(1)}, pred[320]{0:T(512)(128)(4,1)}, u32[]{:S(2)}) copy-start(pred[320]{0:T(512)(128)(4,1)} %get-tuple-element.354) | copy-start | bytes 964
  317.3 132.9 %all-to-all-start.1 = ((f32[16,1,1280]{2,1,0:T(1,128)}), f32[16,1,1280]{2,1,0:T(1,128)}, u32[]{:S(2)}, u32[]{:S(2)}) async-start(f32[16,1,1280]{2,1,0:T(1,128)} %reshape.1992), calls=%async_computation.1 | async-start | bytes 163840 | tf_op jit(solution)/shard_map/all_to_all | solution.py:137
  321.4 17.7 %copy-start.19 = (f32[1,8,8,128]{3,0,2,1:T(1,128)S(1)}, f32[1,8,8,128]{3,0,2,1:T(1,128)}, u32[]{:S(2)}) copy-start(f32[1,8,8,128]{3,0,2,1:T(1,128)} %copy-done.18) | copy-start | bytes 98308
  322.3 127.0 %collective-permute-start.2 = (f32[64,1,64]{2,0,1:T(8,128)}, f32[64,1,64]{2,0,1:T(8,128)}, u32[]{:S(2)}, u32[]{:S(2)}) collective-permute-start(f32[64,1,64]{2,0,1:T(8,128)} %copy.460), channel_id=1, source_target_pairs={{0,16},{16,32},{32,48},{48,64},{64,80},{80,96},{96,112},{112,128},... | collective-permute-start | bytes 49160 | tf_op jit(solution)/shard_map/ppermute | solution.py:16
  324.1 15.1 %copy-start.17 = (f32[1,8,8,128]{3,0,2,1:T(1,128)S(1)}, f32[1,8,8,128]{3,0,2,1:T(1,128)}, u32[]{:S(2)}) copy-start(f32[1,8,8,128]{3,0,2,1:T(1,128)} %copy-done.16) | copy-start | bytes 98308
  324.8 124.5 %collective-permute-start.3 = (f32[64,1,64]{2,0,1:T(8,128)}, f32[64,1,64]{2,0,1:T(8,128)}, u32[]{:S(2)}, u32[]{:S(2)}) collective-permute-start(f32[64,1,64]{2,0,1:T(8,128)} %copy.461), channel_id=1, source_target_pairs={{16,0},{32,16},{48,32},{64,48},{80,64},{96,80},{112,96},{128,112},... | collective-permute-start | bytes 49160 | tf_op jit(solution)/shard_map/ppermute | solution.py:19
  324.8 14.4 %copy-start.15 = (f32[1,8,8,128]{3,0,2,1:T(1,128)S(1)}, f32[1,8,8,128]{3,0,2,1:T(1,128)}, u32[]{:S(2)}) copy-start(f32[1,8,8,128]{3,0,2,1:T(1,128)} %copy-done.14) | copy-start | bytes 98308
  324.9 14.4 %copy-start.13 = (f32[1,8,8,128]{3,0,2,1:T(1,128)S(1)}, f32[1,8,8,128]{3,0,2,1:T(1,128)}, u32[]{:S(2)}) copy-start(f32[1,8,8,128]{3,0,2,1:T(1,128)} %copy-done.12) | copy-start | bytes 98308
  325.7 13.6 %copy-start.86 = (f32[512]{0:T(512)S(1)}, f32[512]{0:T(512)}, u32[]{:S(2)}) copy-start(f32[512]{0:T(512)} %mul.2626) | copy-start | bytes 6148
  325.7 13.6 %copy-start.87 = (f32[512]{0:T(512)S(1)}, f32[512]{0:T(512)}, u32[]{:S(2)}) copy-start(f32[512]{0:T(512)} %mul.2634) | copy-start | bytes 6148
  325.7 13.6 %copy-start.88 = (f32[512]{0:T(512)S(1)}, f32[512]{0:T(512)}, u32[]{:S(2)}) copy-start(f32[512]{0:T(512)} %mul.2642) | copy-start | bytes 6148
  325.7 13.6 %copy-start.89 = (f32[512]{0:T(512)S(1)}, f32[512]{0:T(512)}, u32[]{:S(2)}) copy-start(f32[512]{0:T(512)} %mul.2650) | copy-start | bytes 6148
  325.7 13.6 %copy-start.90 = (f32[512]{0:T(512)S(1)}, f32[512]{0:T(512)}, u32[]{:S(2)}) copy-start(f32[512]{0:T(512)} %mul.2658) | copy-start | bytes 6148
  325.7 13.6 %copy-start.91 = (f32[512]{0:T(512)S(1)}, f32[512]{0:T(512)}, u32[]{:S(2)}) copy-start(f32[512]{0:T(512)} %mul.2666) | copy-start | bytes 6148
  325.7 13.6 %copy-start.92 = (f32[512]{0:T(512)S(1)}, f32[512]{0:T(512)}, u32[]{:S(2)}) copy-start(f32[512]{0:T(512)} %mul.2674) | copy-start | bytes 6148
  325.7 13.6 %copy-start.93 = (f32[512]{0:T(512)S(1)}, f32[512]{0:T(512)}, u32[]{:S(2)}) copy-start(f32[512]{0:T(512)} %mul.2682) | copy-start | bytes 6148
  325.7 13.6 %copy-start.94 = (f32[512]{0:T(512)S(1)}, f32[512]{0:T(512)}, u32[]{:S(2)}) copy-start(f32[512]{0:T(512)} %mul.2690) | copy-start | bytes 6148
  339.5 108.0 %copy-start.72 = (f32[128]{0:T(128)S(1)}, f32[128]{0:T(128)}, u32[]{:S(2)}) copy-start(f32[128]{0:T(128)} %copy-done.71) | copy-start | bytes 1540
  339.5 110.6 %copy-start.67 = (pred[128]{0:T(512)(128)(4,1)S(1)}, pred[128]{0:T(512)(128)(4,1)}, u32[]{:S(2)}) copy-start(pred[128]{0:T(512)(128)(4,1)} %copy-done.66) | copy-start | bytes 388
  339.6 110.6 %copy-start.84 = (pred[128]{0:T(512)(128)(4,1)S(1)}, pred[128]{0:T(512)(128)(4,1)}, u32[]{:S(2)}) copy-start(pred[128]{0:T(512)(128)(4,1)} %get-tuple-element.361) | copy-start | bytes 388
  339.6 110.6 %copy-start.118 = (pred[128]{0:T(512)(128)(4,1)S(1)}, pred[128]{0:T(512)(128)(4,1)}, u32[]{:S(2)}) copy-start(pred[128]{0:T(512)(128)(4,1)} %get-tuple-element.359) | copy-start | bytes 388
  339.6 112.4 %copy-start.123 = (pred[16]{0:T(512)(128)(4,1)S(1)}, pred[16]{0:T(512)(128)(4,1)}, u32[]{:S(2)}) copy-start(pred[16]{0:T(512)(128)(4,1)} %iota_compare_fusion.2) | copy-start | bytes 52
  342.5 110.2 %copy-start.65 = (pred[320]{0:T(512)(128)(4,1)S(1)}, pred[320]{0:T(512)(128)(4,1)}, u32[]{:S(2)}) copy-start(pred[320]{0:T(512)(128)(4,1)} %get-tuple-element.355) | copy-start | bytes 964
  342.5 110.4 %copy-start.74 = (pred[320]{0:T(512)(128)(4,1)S(1)}, pred[320]{0:T(512)(128)(4,1)}, u32[]{:S(2)}) copy-start(pred[320]{0:T(512)(128)(4,1)} %get-tuple-element.356) | copy-start | bytes 964
  342.5 110.4 %copy-start.112 = (pred[320]{0:T(512)(128)(4,1)S(1)}, pred[320]{0:T(512)(128)(4,1)}, u32[]{:S(2)}) copy-start(pred[320]{0:T(512)(128)(4,1)} %get-tuple-element.354) | copy-start | bytes 964
  (84 other events, 478.0 us)
where the time goes:
time: 570 us; the launch traced here: 567 us
  blocking collectives  410 us (72%)
  local copies, waits for them, and re-layouts  94 us (16%)
  other arithmetic  34.3 us (6%)
  starting transfers between devices  17 us (3%)
  between operations  9.18 us (2%)
    psum x1, blocking collectives, on_device(): coarse_rhs = lax.psum(coarse_partial, ('gx', 'gy'))  109 us
    psum x1, blocking collectives, on_device(): lax.psum((precond_local, curvature_local, norm_local), ('gx', 'gy'))  102 us
    unnamed x1, blocking collectives  99.5 us
    psum x1, blocking collectives, on_device(): fresh_norm = lax.psum(jnp.sum(residual_out * residual_out), ('gx', 'gy'))  99.4 us
    mul x78, local copies, waits for them, and re-layouts, contract(): total = total + matrices[index][:, None, None, :] * moved[index][None]  28.3 us
    unnamed x280, local copies, waits for them, and re-layouts  12 us
    all_to_all x2, starting transfers between devices, face_sum(): lax.all_to_all(outgoing, 'gy', split_axis=1, concat_axis=1, tiled=True)  11.8 us
  transfers between devices with their start and end apart: 6, of which 0 were waited for; matrix products, arithmetic and copies ran while one was open for 12% of the time, Pallas kernels for 0%

commit v1 on v0

--- a/solution.py
+++ b/solution.py
@@ -134,7 +134,10 @@
         EDGE * EDGE, peer_count, capacity
     )
     own_index = lax.axis_index("gy")
-    arrived = lax.all_to_all(outgoing, "gy", split_axis=1, concat_axis=1, tiled=True)
+    arrived = jnp.concatenate(
+        lax.all_to_all(jnp.stack(jnp.split(outgoing, lax.axis_size("gy"), axis=1)), "gy", 0, 0),
+        axis=1,
+    )
     swapped = arrived.reshape(EDGE * EDGE, peer_count, capacity // 2, 2)[..., ::-1].reshape(
         EDGE * EDGE, peer_count, capacity
     )

time: 570 us -> 587 us (1.030)
  other arithmetic: 34.3 us -> 49.6 us
    mul x78, local copies, waits for them, and re-layouts: 28.3 us -> 16.5 us  [contract(): total = total + matrices[index][:, None, None, :] * moved[index][None]]
    select_n x0 -> x2, other arithmetic: none -> 6.09 us  [orient_columns(): jnp.where((orient_codes >= 4)[None, None, :], jnp.swapaxes(face_grid, 0,...]
    unnamed x280 -> x339, local copies, waits for them, and re-layouts: 12 us -> 15.2 us
  transfers between devices with their start and end apart: 6 -> 6, of which waited for: 0 -> 0; matrix products, arithmetic and copies ran while one was open for 12% -> 8% of each run, Pallas kernels for 0% -> 0%
where the time goes in v1:
time: 587 us; the launch traced here: 579 us
  blocking collectives  411 us (70%)
  local copies, waits for them, and re-layouts  89.7 us (15%)
  other arithmetic  49.6 us (8%)
  starting transfers between devices  16 us (3%)
  between operations  9.68 us (2%)
    psum x1, blocking collectives, on_device(): coarse_rhs = lax.psum(coarse_partial, ('gx', 'gy'))  109 us
    psum x1, blocking collectives, on_device(): lax.psum((precond_local, curvature_local, norm_local), ('gx', 'gy'))  103 us
    unnamed x1, blocking collectives  99.8 us
    psum x1, blocking collectives, on_device(): fresh_norm = lax.psum(jnp.sum(residual_out * residual_out), ('gx', 'gy'))  99 us
    mul x78, local copies, waits for them, and re-layouts, contract(): total = total + matrices[index][:, None, None, :] * moved[index][None]  16.5 us
    unnamed x339, local copies, waits for them, and re-layouts  15.2 us
  transfers between devices with their start and end apart: 6, of which 0 were waited for; matrix products, arithmetic and copies ran while one was open for 8% of the time, Pallas kernels for 0%

profile of v1, /device:TPU:1, one launch (start us, length us, event | category | flops | bytes accessed | tf_op | source)
XLA Modules:
  0.0 578.6 jit_solution(2032918064592078883)
XLA Ops:
  3.8 1.0 broadcast_multiply_fusion.3
  6.7 2.2 copy.409
  8.9 2.4 reshape.1881
  12.4 1.1 gather_fusion.1
  16.3 7.7 %all-to-all-start = ((f32[16,1,1280]{2,1,0:T(1,128)}), f32[16,1,1280]{2,1,0:T(1,128)S(1)}, u32[]{:S(2)}, u32[]{:S(2)}) async-start(f32[16,1,1280]{2,1,0:T(1,128)} %reshape.2006), calls=%async_computation | async-start | bytes 163840 | tf_op jit(solution)/shard_map/all_to_all | solution.py:138
  25.0 2.5 collective-permute-start
  30.2 5.9 %scatter_custom_fusion.1 = f32[8192]{0:T(1024)S(1)} fusion(s32[1024]{0:T(1024)S(1)} %bitcast.793, f32[1024]{0:T(1024)S(1)} %convolution_bitcast_fusion, f32[]{:T(128)} %constant.402.clone.1), kind=kCustom, calls=%fused_computation.229 | custom fusion | flops 1024 | bytes 32772 | tf_op jit(solution)/shard_map/scatter-add | solution.py:194
  36.2 109.2 %psum.35 = f32[8192]{0:T(1024)S(1)} all-reduce(f32[8192]{0:T(1024)S(1)} %scatter_custom_fusion.1), channel_id=1, replica_groups=mesh['gx'=32,'gy'=16] {'gx','gy'}, use_global_device_ids=true, to_apply=%region_2.5 | all-reduce | flops 8192 | bytes 65536 | tf_op jit(solution)/shard_map/psum | solution.py:197
  171.6 99.8 %all-reduce = f32[8192]{0:T(1024)S(1)} all-reduce(f32[8192]{0:T(1024)S(1)} %dynamic-update-slice.36), channel_id=1, replica_groups=mesh['gx'=32,'gy'=16] {'gx','gy'}, use_global_device_ids=true, to_apply=%add | all-reduce | flops 8192 | bytes 65536
  271.4 6.1 %gather_fusion = f32[1024]{0:T(1024)S(1)} fusion(f32[8192]{0:T(1024)S(1)} %all-reduce, s32[1024]{0:T(1024)S(1)} %fusion.34), kind=kCustom, calls=%fused_computation.4 | custom fusion | bytes 12288 | tf_op jit(solution)/shard_map/gather | solution.py:204
  279.4 1.4 reshape.1998
  280.8 2.2 broadcast_select_fusion.1
  283.0 1.7 rev.31
  284.7 2.2 broadcast_select_fusion.3
  286.9 2.0 rev.32
  288.9 2.2 broadcast_select_fusion.5
  291.8 1.9 bitcast_select_fusion
  293.7 1.7 copy.416
  295.7 2.9 scatter_custom_fusion
  298.6 1.9 reshape.1889
  300.5 1.7 fusion.48
  302.3 1.3 copy.486
  303.6 1.2 copy.487
  304.8 1.2 copy.424
  308.4 1.2 multiply_reduce_fusion
  317.3 2.0 copy.451
  319.4 1.6 reshape.1899
  321.0 2.1 gather_fusion.3
  323.1 1.8 gather_fusion.4
  325.4 1.0 reduce.28
  327.2 4.0 all-to-all-start.1
  331.4 1.5 collective-permute-start.2
  335.7 2.9 add_reduce_fusion
  339.8 103.4 %all-reduce.2 = (f32[]{:T(128)}, f32[]{:T(128)}) all-reduce(f32[]{:T(128)} %get-tuple-element.150, f32[]{:T(128)S(6)} %add.970), channel_id=1, replica_groups=mesh['gx'=32,'gy'=16] {'gx','gy'}, use_global_device_ids=true, to_apply=%region_4.7 | all-reduce | flops 2 | bytes 16 | tf_op jit(solution)/shard_map/psum | solution.py:210
  447.0 1.5 reshape.1999
  448.5 2.2 broadcast_select_fusion
  450.7 1.7 rev.36
  452.3 2.2 broadcast_select_fusion.2
  455.5 1.9 fusion.1
  457.4 2.8 copy.457
  460.2 4.2 broadcast_select_fusion.6
  464.4 1.7 copy.458
  466.4 2.3 scatter_custom_fusion.2
  469.6 1.7 fusion.47
  471.3 1.3 copy.492
  472.7 1.3 copy.493
  475.5 1.3 multiply_reduce_fusion.1
  476.9 99.0 %all-reduce.1 = (f32[]{:T(128)}, f32[]{:T(128)}) all-reduce(f32[]{:T(128)} %get-tuple-element.156, f32[]{:T(128)} %get-tuple-element.149), channel_id=1, replica_groups=mesh['gx'=32,'gy'=16] {'gx','gy'}, use_global_device_ids=true, to_apply=%region_11.14 | all-reduce | flops 2 | bytes 16 | tf_op jit(solution)/shard_map/psum | solution.py:215
  (575 shorter events, 58.8 us)
Async XLA Ops:
  0.6 148.2 %copy-start = (f32[16,8192]{1,0:T(8,128)S(1)}, f32[16,8192]{1,0:T(8,128)}, u32[]{:S(2)}) copy-start(f32[16,8192]{1,0:T(8,128)} %param.48) | copy-start | bytes 1572868
  4.8 25.2 %copy-start.2 = (f32[512,128]{1,0:T(8,128)}, f32[512,128]{1,0:T(8,128)S(1)}, u32[]{:S(2)}) copy-start(f32[512,128]{1,0:T(8,128)S(1)} %broadcast_multiply_fusion.3) | copy-start | bytes 786436
  12.2 3.2 copy-start.129
  12.3 3.1 copy-start.131
  12.4 3.1 copy-start.76
  12.4 11.6 %copy-start.122 = (s32[1024]{0:T(1024)}, s32[1024]{0:T(1024)S(1)}, u32[]{:S(2)}) copy-start(s32[1024]{0:T(1024)S(1)} %get-tuple-element.377) | copy-start | bytes 12292
  13.5 11.2 %copy-start.138 = (s32[1,2,64]{2,1,0:T(2,128)S(1)}, s32[1,2,64]{2,1,0:T(2,128)}, u32[]{:S(2)}) copy-start(s32[1,2,64]{2,1,0:T(2,128)} %param.53) | copy-start | bytes 1540
  15.5 14.7 %copy-start.137 = (s32[8,128]{1,0:T(8,128)S(1)}, s32[8,128]{1,0:T(8,128)}, u32[]{:S(2)}) copy-start(s32[8,128]{1,0:T(8,128)} %param.47) | copy-start | bytes 12292
  16.3 129.4 %copy-start.5 = (bf16[3,512,128]{2,1,0:T(8,128)(2,1)S(1)}, bf16[3,512,128]{2,1,0:T(8,128)(2,1)}, u32[]{:S(2)}) copy-start(bf16[3,512,128]{2,1,0:T(8,128)(2,1)} %param.44) | copy-start | bytes 1179652
  16.3 261.5 %all-to-all-start = ((f32[16,1,1280]{2,1,0:T(1,128)}), f32[16,1,1280]{2,1,0:T(1,128)S(1)}, u32[]{:S(2)}, u32[]{:S(2)}) async-start(f32[16,1,1280]{2,1,0:T(1,128)} %reshape.2006), calls=%async_computation | async-start | bytes 163840 | tf_op jit(solution)/shard_map/all_to_all | solution.py:138
  24.8 3.1 copy-start.135
  24.8 252.9 %copy-start.74 = (pred[128]{0:T(512)(128)(4,1)}, pred[128]{0:T(512)(128)(4,1)S(1)}, u32[]{:S(2)}) copy-start(pred[128]{0:T(512)(128)(4,1)S(1)} %get-tuple-element.364) | copy-start | bytes 388
  24.8 252.9 %copy-start.95 = (pred[128]{0:T(512)(128)(4,1)}, pred[128]{0:T(512)(128)(4,1)S(1)}, u32[]{:S(2)}) copy-start(pred[128]{0:T(512)(128)(4,1)S(1)} %get-tuple-element.365) | copy-start | bytes 388
  24.8 252.9 %copy-start.133 = (pred[128]{0:T(512)(128)(4,1)}, pred[128]{0:T(512)(128)(4,1)S(1)}, u32[]{:S(2)}) copy-start(pred[128]{0:T(512)(128)(4,1)S(1)} %get-tuple-element.363) | copy-start | bytes 388
  25.0 252.6 %collective-permute-start = (f32[64,1,64]{2,0,1:T(8,128)S(1)}, f32[64,1,64]{2,0,1:T(8,128)S(1)}, u32[]{:S(2)}, u32[]{:S(2)}) collective-permute-start(f32[64,1,64]{2,0,1:T(8,128)S(1)} %copy.484), channel_id=1, source_target_pairs={{0,16},{16,32},{32,48},{48,64},{64,80},{80,96},{96,112},{112,128},... | collective-permute-start | bytes 49160 | tf_op jit(solution)/shard_map/ppermute | solution.py:16
  27.6 250.0 %collective-permute-start.1 = (f32[64,1,64]{2,0,1:T(8,128)S(1)}, f32[64,1,64]{2,0,1:T(8,128)S(1)}, u32[]{:S(2)}, u32[]{:S(2)}) collective-permute-start(f32[64,1,64]{2,0,1:T(8,128)S(1)} %copy.485), channel_id=1, source_target_pairs={{16,0},{32,16},{48,32},{64,48},{80,64},{96,80},{112,96},{128,112},... | collective-permute-start | bytes 49160 | tf_op jit(solution)/shard_map/ppermute | solution.py:19
  29.5 117.1 %copy-start.4 = (bf16[3,512,128]{2,1,0:T(8,128)(2,1)S(1)}, bf16[3,512,128]{2,1,0:T(8,128)(2,1)}, u32[]{:S(2)}) copy-start(bf16[3,512,128]{2,1,0:T(8,128)(2,1)} %param.43) | copy-start | bytes 1179652
  145.7 21.0 %copy-start.71 = (f32[8]{0:T(128)}, f32[8]{0:T(128)S(1)}, u32[]{:S(2)}) copy-start(f32[8]{0:T(128)S(1)} %get-tuple-element.357) | copy-start | bytes 100
  145.7 21.7 %copy-start.69 = (f32[8]{0:T(128)}, f32[8]{0:T(128)S(1)}, u32[]{:S(2)}) copy-start(f32[8]{0:T(128)S(1)} %get-tuple-element.356) | copy-start | bytes 100
  145.7 22.3 %copy-start.67 = (f32[8]{0:T(128)}, f32[8]{0:T(128)S(1)}, u32[]{:S(2)}) copy-start(f32[8]{0:T(128)S(1)} %get-tuple-element.355) | copy-start | bytes 100
  145.7 23.0 %copy-start.65 = (f32[8]{0:T(128)}, f32[8]{0:T(128)S(1)}, u32[]{:S(2)}) copy-start(f32[8]{0:T(128)S(1)} %get-tuple-element.354) | copy-start | bytes 100
  302.2 3.8 copy-start.19
  302.2 4.0 copy-start.18
  302.2 4.2 copy-start.16
  303.6 3.1 copy-start.79
  303.6 3.1 copy-start.80
  313.5 3.2 copy-start.6
  319.4 5.5 copy-start.130
  319.4 5.5 copy-start.132
  323.0 8.1 %copy-start.136 = (pred[128]{0:T(512)(128)(4,1)S(1)}, pred[128]{0:T(512)(128)(4,1)}, u32[]{:S(2)}) copy-start(pred[128]{0:T(512)(128)(4,1)} %copy-done.135) | copy-start | bytes 388
  324.8 8.2 %copy-start.57 = (f32[8,8,128]{2,1,0:T(8,128)S(1)}, f32[8,8,128]{2,1,0:T(8,128)}, u32[]{:S(2)}) copy-start(f32[8,8,128]{2,1,0:T(8,128)} %copy-done.56) | copy-start | bytes 98308
  325.0 8.0 %copy-start.53 = (f32[8,8,128]{2,1,0:T(8,128)S(1)}, f32[8,8,128]{2,1,0:T(8,128)}, u32[]{:S(2)}) copy-start(f32[8,8,128]{2,1,0:T(8,128)} %copy-done.52) | copy-start | bytes 98308
  325.0 8.0 %copy-start.49 = (f32[8,8,128]{2,1,0:T(8,128)S(1)}, f32[8,8,128]{2,1,0:T(8,128)}, u32[]{:S(2)}) copy-start(f32[8,8,128]{2,1,0:T(8,128)} %copy-done.48) | copy-start | bytes 98308
  325.1 8.0 %copy-start.45 = (f32[8,8,128]{2,1,0:T(8,128)S(1)}, f32[8,8,128]{2,1,0:T(8,128)}, u32[]{:S(2)}) copy-start(f32[8,8,128]{2,1,0:T(8,128)} %copy-done.44) | copy-start | bytes 98308
  325.2 7.9 %copy-start.41 = (f32[8,8,128]{2,1,0:T(8,128)S(1)}, f32[8,8,128]{2,1,0:T(8,128)}, u32[]{:S(2)}) copy-start(f32[8,8,128]{2,1,0:T(8,128)} %copy-done.40) | copy-start | bytes 98308
  325.4 7.8 %copy-start.37 = (f32[8,8,128]{2,1,0:T(8,128)S(1)}, f32[8,8,128]{2,1,0:T(8,128)}, u32[]{:S(2)}) copy-start(f32[8,8,128]{2,1,0:T(8,128)} %copy-done.36) | copy-start | bytes 98308
  326.4 6.9 %copy-start.35 = (f32[8,8,128]{2,1,0:T(8,128)S(1)}, f32[8,8,128]{2,1,0:T(8,128)}, u32[]{:S(2)}) copy-start(f32[8,8,128]{2,1,0:T(8,128)} %copy-done.34) | copy-start | bytes 98308
  327.2 6.1 %copy-start.33 = (f32[8,8,128]{2,1,0:T(8,128)S(1)}, f32[8,8,128]{2,1,0:T(8,128)}, u32[]{:S(2)}) copy-start(f32[8,8,128]{2,1,0:T(8,128)} %copy-done.32) | copy-start | bytes 98308
  327.2 118.2 %all-to-all-start.1 = ((f32[16,1,1280]{2,1,0:T(1,128)}), f32[16,1,1280]{2,1,0:T(1,128)S(1)}, u32[]{:S(2)}, u32[]{:S(2)}) async-start(f32[16,1,1280]{2,1,0:T(1,128)} %reshape.2008), calls=%async_computation.1 | async-start | bytes 163840 | tf_op jit(solution)/shard_map/all_to_all | solution.py:138
  331.4 113.8 %collective-permute-start.2 = (f32[64,1,64]{2,0,1:T(8,128)S(1)}, f32[64,1,64]{2,0,1:T(8,128)S(1)}, u32[]{:S(2)}, u32[]{:S(2)}) collective-permute-start(f32[64,1,64]{2,0,1:T(8,128)S(1)} %copy.490), channel_id=1, source_target_pairs={{0,16},{16,32},{32,48},{48,64},{64,80},{80,96},{96,112},{112,128},... | collective-permute-start | bytes 49160 | tf_op jit(solution)/shard_map/ppermute | solution.py:16
  333.0 112.2 %collective-permute-start.3 = (f32[64,1,64]{2,0,1:T(8,128)S(1)}, f32[64,1,64]{2,0,1:T(8,128)S(1)}, u32[]{:S(2)}, u32[]{:S(2)}) collective-permute-start(f32[64,1,64]{2,0,1:T(8,128)S(1)} %copy.491), channel_id=1, source_target_pairs={{16,0},{32,16},{48,32},{64,48},{80,64},{96,80},{112,96},{128,112},... | collective-permute-start | bytes 49160 | tf_op jit(solution)/shard_map/ppermute | solution.py:19
  335.7 108.8 %copy-start.64 = (f32[512,128]{1,0:T(8,128)S(1)}, f32[512,128]{1,0:T(8,128)}, u32[]{:S(2)}) copy-start(f32[512,128]{1,0:T(8,128)} %param.41) | copy-start | bytes 786436
  335.7 108.8 %copy-start.84 = (f32[128]{0:T(128)S(1)}, f32[128]{0:T(128)}, u32[]{:S(2)}) copy-start(f32[128]{0:T(128)} %copy-done.82) | copy-start | bytes 1540
  335.7 109.6 %copy-start.75 = (pred[128]{0:T(512)(128)(4,1)S(1)}, pred[128]{0:T(512)(128)(4,1)}, u32[]{:S(2)}) copy-start(pred[128]{0:T(512)(128)(4,1)} %copy-done.74) | copy-start | bytes 388
  335.7 109.6 %copy-start.96 = (pred[128]{0:T(512)(128)(4,1)S(1)}, pred[128]{0:T(512)(128)(4,1)}, u32[]{:S(2)}) copy-start(pred[128]{0:T(512)(128)(4,1)} %copy-done.95) | copy-start | bytes 388
  335.7 109.6 %copy-start.134 = (pred[128]{0:T(512)(128)(4,1)S(1)}, pred[128]{0:T(512)(128)(4,1)}, u32[]{:S(2)}) copy-start(pred[128]{0:T(512)(128)(4,1)} %copy-done.133) | copy-start | bytes 388
  471.3 3.5 copy-start.14
  474.8 102.4 %copy-start.1 = (f32[16,8192]{1,0:T(8,128)S(1)}, f32[16,8192]{1,0:T(8,128)}, u32[]{:S(2)}) copy-start(f32[16,8192]{1,0:T(8,128)} %param.48) | copy-start | bytes 1572868
  (98 other events, 156.3 us)
